TPU v7x, 256 devices: a whole 4x4x8 slice. The times are simulated.
256 devices in a mesh: blk: 32 (over x, z_hi, core), walker: 8 (over y, z_lo).
Axes of the slice: x: 4, y: 4, z: 8 (z_hi: 4, z_lo: 2; z = z_hi * 2 + z_lo), core: 2. Of those that a mesh axis runs over, the one named last changes fastest.
Arguments:
- measured: bfloat16 [1024, 2, 2, 1440], P(('blk', 'walker')), may hold values from -6 to 6
- slice_q: int32 [64], replicated, may hold values from 0 to 35, as said below
- slice_nu: int32 [64], replicated, may hold values from 0 to 7
- kplusq: int32 [36, 36], replicated, may hold values from 0 to 35, as said below
Outputs:
- four_point: float32 [1152, 64, 2, 1152], P('walker', 'blk')
Inputs may be any that keep to these rules, and one draw needn't show every extreme that they name: slice_q takes 8 distinct momenta and slice_nu all 8 bosonic frequencies; every pair of them is one slice, once. kplusq is the addition table of a 6 x 6 periodic momentum grid under a relabelling of the momenta: each row and each column holds every label once, it is symmetric and associative.
All inputs are finite; a program needn't handle non-finite values.
Results may differ from a plain program's by a relative error of at most 0.0003.
Values may be sent and summed in bfloat16 or wider, within the bound.
A program may use at most 128 MiB of HBM per device.

v0:
```python
import jax
import jax.numpy as jnp
from jax import lax
from jax.sharding import PartitionSpec as P

VERTEX_FREQS = 32


def shards(measured, slice_q, slice_nu, kplusq):
    block_count = lax.axis_size("blk")
    walker_count = lax.axis_size("walker")
    momenta = kplusq.shape[0]
    width = measured.shape[-1]
    freq_green = width // momenta
    ncw = momenta * VERTEX_FREQS
    per_dev = slice_q.shape[0] // block_count
    own_rows = ncw // walker_count
    measurement_total = measured.shape[0] * block_count * walker_count
    norm_scale = (2.0 * measurement_total) ** (-0.5)
    owned_q = lax.dynamic_slice_in_dim(slice_q, lax.axis_index("blk") * per_dev, per_dev)
    owned_nu = lax.dynamic_slice_in_dim(slice_nu, lax.axis_index("blk") * per_dev, per_dev)
    pairs = jnp.arange(ncw, dtype=jnp.int32)
    k_of = pairs // VERTEX_FREQS
    w_of = pairs % VERTEX_FREQS
    col_index = (
        jnp.transpose(kplusq[k_of][:, owned_q]) * freq_green + w_of[None, :] + owned_nu[:, None]
    )
    row_pairs = lax.axis_index("walker") * own_rows + jnp.arange(own_rows, dtype=jnp.int32)
    row_index = row_pairs // VERTEX_FREQS * freq_green + row_pairs % VERTEX_FREQS
    piece = lax.all_gather(measured, ("blk", "walker"), axis=0, tiled=True)
    count = piece.shape[0]
    rows = jnp.take(piece, row_index, axis=3)
    left_factor = jnp.concatenate(
        [rows[:, :, 0].reshape(count * 2, own_rows), rows[:, :, 1].reshape(count * 2, own_rows)],
        axis=0,
    )
    results = []
    for slot in range(per_dev):
        cols = jnp.take(piece, col_index[slot], axis=3)
        product_real = cols[:, :, 0].reshape(count * 2, ncw)
        product_imaginary = cols[:, :, 1].reshape(count * 2, ncw)
        right = jnp.concatenate(
            [
                jnp.concatenate([product_real, product_imaginary], axis=1),
                jnp.concatenate([-product_imaginary, product_real], axis=1),
            ],
            axis=0,
        )
        results.append(
            jnp.einsum("kr,kc->rc", left_factor, right, preferred_element_type=jnp.float32)
        )
    result = jnp.stack(results, axis=1) * norm_scale
    return result.reshape(own_rows, per_dev, 2, ncw)


def solution(mesh):
    return jax.shard_map(
        shards,
        mesh=mesh,
        in_specs=(P(("blk", "walker"), None, None, None), P(), P(), P()),
        out_specs=P("walker", "blk", None, None),
        check_vma=False,
    )
```

profile of v0, /device:TPU:1, one launch (start us, length us, event | category | flops | bytes accessed | tf_op | source)
XLA Modules:
  0.0 1126.1 jit_solution(2802222824462487104)
XLA Ops:
  11.0 728.5 %all-gather.2.cloned.1.call-done = bf16[1024,2,2,1440]{3,2,1,0:T(2,128)(2,1)} async-done(((bf16[4,2,2,1440]{3,2,1,0:T(2,128)(2,1)}), bf16[1024,2,2,1440]{3,2,1,0:T(2,128)(2,1)}) %all-gather.2.cloned.1.call-update) | async-done | bytes 11796496 | tf_op jit(solution)/shard_map/all_gather | solution.py:30
  739.5 57.5 %copy.18 = bf16[1024,2,2,1440]{0,1,2,3:T(2,128)(2,1)} copy(bf16[1024,2,2,1440]{3,2,1,0:T(2,128)(2,1)} %all-gather.2.cloned.1.call-done) | data formatting | bytes 23592960 | tf_op jit(solution)/shard_map/all_gather | solution.py:30
  797.0 43.5 %gather_fusion.3 = bf16[1152,1024,2,2]{1,2,3,0:T(2,128)(2,1)} fusion(bf16[1024,2,2,1440]{0,1,2,3:T(2,128)(2,1)} %copy.18, s32[2048]{0:T(1024)S(1)} %pad_clamp_fusion.1), kind=kCustom, calls=%fused_computation.clone | custom fusion | bytes 18878976 | tf_op jit(solution)/shard_map/jit(_take)/gather | solution.py:39
  840.5 13.6 %fusion.16 = bf16[1024,2,2,1152]{0,1,2,3:T(2,128)(2,1)S(1)} fusion(bf16[1152,1024,2,2]{1,2,3,0:T(2,128)(2,1)} %gather_fusion.3, pred[1152]{0:T(1024)(128)(4,1)S(1)} %get-tuple-element.17), kind=kLoop, calls=%fused_computation.23 | loop fusion | flops 4718592 | bytes 18875520 | tf_op jit(solution)/shard_map/jit(_take)/select_n | solution.py:39
  854.1 7.7 fusion.27
  861.8 16.1 %copy.24 = bf16[1024,2,1,1152]{3,1,0,2:T(2,128)(2,1)} copy(bf16[1024,2,1,1152]{0,1,2,3:T(2,128)(2,1)} %get-tuple-element.8) | data formatting | bytes 9437184 | tf_op jit(solution)/shard_map/slice | solution.py:41
  877.9 10.7 reshape_squeeze.21
  888.6 5.4 neg.6
  894.0 16.2 %copy.23 = bf16[1024,2,1,1152]{3,1,0,2:T(2,128)(2,1)} copy(bf16[1024,2,1,1152]{0,1,2,3:T(2,128)(2,1)} %get-tuple-element.9) | data formatting | bytes 9437184 | tf_op jit(solution)/shard_map/slice | solution.py:40
  910.2 10.7 reshape_squeeze.20
  920.9 15.5 %gather_fusion = bf16[144,1024,2,2]{1,2,3,0:T(2,128)(2,1)S(1)} fusion(bf16[1024,2,2,1440]{0,1,2,3:T(2,128)(2,1)} %copy.18, s32[1024]{0:T(1024)S(1)} %pad_clamp_fusion.4), kind=kCustom, calls=%fused_computation.2 | custom fusion | bytes 2359872 | tf_op jit(solution)/shard_map/jit(_take)/gather | solution.py:32
  938.4 2.7 copy.19
  943.2 2.7 copy.20
  948.0 19.9 %fusion = f32[144,2304]{1,0:T(8,128)S(1)} fusion(bf16[4096,144]{1,0:T(8,128)(2,1)} %constant_dynamic-update-slice_fusion, bf16[2048,1152]{1,0:T(8,128)(2,1)} %reshape_squeeze.20, bf16[2048,1152]{1,0:T(8,128)(2,1)} %neg.6, bf16[2048,1152]{1,0:T(8,128)(2,1)} %reshape_squeeze.21), kind=kOutput, calls=%fused_computation.5 | convolution fusion | flops 2793406464 | bytes 16662528 | tf_op jit(solution)/shard_map/kr,kc->rc/dot_general | solution.py:50
  968.6 43.5 %gather_fusion.4 = bf16[1152,1024,2,2]{1,2,3,0:T(2,128)(2,1)} fusion(bf16[1024,2,2,1440]{0,1,2,3:T(2,128)(2,1)} %copy.18, s32[2048]{0:T(1024)S(1)} %pad_clamp_fusion), kind=kCustom, calls=%fused_computation.1.clone | custom fusion | bytes 18878976 | tf_op jit(solution)/shard_map/jit(_take)/gather | solution.py:39
  1012.1 13.6 %fusion.17 = bf16[1024,2,2,1152]{0,1,2,3:T(2,128)(2,1)S(1)} fusion(bf16[1152,1024,2,2]{1,2,3,0:T(2,128)(2,1)} %gather_fusion.4, pred[1152]{0:T(1024)(128)(4,1)S(1)} %get-tuple-element.16), kind=kLoop, calls=%fused_computation.24 | loop fusion | flops 4718592 | bytes 18875520 | tf_op jit(solution)/shard_map/jit(_take)/select_n | solution.py:39
  1025.7 7.7 fusion.28
  1033.4 16.1 %copy.27 = bf16[1024,2,1,1152]{3,1,0,2:T(2,128)(2,1)} copy(bf16[1024,2,1,1152]{0,1,2,3:T(2,128)(2,1)} %get-tuple-element.10) | data formatting | bytes 9437184 | tf_op jit(solution)/shard_map/slice | solution.py:41
  1049.5 10.9 reshape_squeeze.23
  1060.5 5.5 neg.7
  1065.9 16.2 %copy.26 = bf16[1024,2,1,1152]{3,1,0,2:T(2,128)(2,1)} copy(bf16[1024,2,1,1152]{0,1,2,3:T(2,128)(2,1)} %get-tuple-element.11) | data formatting | bytes 9437184 | tf_op jit(solution)/shard_map/slice | solution.py:40
  1082.1 10.9 reshape_squeeze.22
  1093.0 20.7 %fusion.8 = f32[144,2304]{1,0:T(8,128)} fusion(bf16[4096,144]{1,0:T(8,128)(2,1)S(1)} %copy-done.2, bf16[2048,1152]{1,0:T(8,128)(2,1)} %reshape_squeeze.22, bf16[2048,1152]{1,0:T(8,128)(2,1)} %neg.7, bf16[2048,1152]{1,0:T(8,128)(2,1)} %reshape_squeeze.23), kind=kOutput, calls=%fused_computation.13 | convolution fusion | flops 2793406464 | bytes 16662528 | tf_op jit(solution)/shard_map/kr,kc->rc/dot_general | solution.py:50
  1115.8 3.2 maximum_multiply_fusion
  (38 shorter events, 13.2 us)
Async XLA Ops:
  6.5 0.8 copy-start
  6.5 3.5 copy-start.3
  6.5 3.6 copy-start.4
  6.5 732.9 %all-gather.2.cloned.1.call-start = ((), (), s32[]{:S(2)}) async-start(), calls=%async_computation | async-start | bytes 12632064 | tf_op jit(solution)/shard_map/all_gather | solution.py:30
  1082.1 10.9 copy-start.2
  1093.0 26.0 %copy-start.1 = (s32[36,36]{1,0:T(8,128)S(1)}, s32[36,36]{1,0:T(8,128)}, u32[]{:S(2)}) copy-start(s32[36,36]{1,0:T(8,128)} %param.9) | copy-start | bytes 15556
Sparse Core Ops, SparseCore 0:
  9.2 730.1 all-gather.1
where the time goes:
time: 1140 us; the launch traced here: 1130 us
  waiting for transfers between devices  729 us (64%)
  local copies, waits for them, and re-layouts  300 us (26%)
  other arithmetic  42.6 us (4%)
  matrix products  40.6 us (4%)
  between operations  13.8 us (1%)
    all_gather x1, waiting for transfers between devices, shards(): piece = lax.all_gather(measured, ('blk', 'walker'), axis=0, tiled=True)  728 us
    gather x2, local copies, waits for them, and re-layouts, shards(): cols = jnp.take(piece, col_index[slot], axis=3)  87.1 us
    all_gather x1, local copies, waits for them, and re-layouts, shards(): piece = lax.all_gather(measured, ('blk', 'walker'), axis=0, tiled=True)  57.5 us
    slice x4, local copies, waits for them, and re-layouts, shards(): product_imaginary = cols[:, :, 1].reshape(count * 2, ncw)  47.6 us
    dot_general x2, matrix products, shards(): jnp.einsum('kr,kc->rc', left_factor, right, preferred_element_type=jnp.fl...  40.6 us
    slice x2, local copies, waits for them, and re-layouts, shards(): product_real = cols[:, :, 0].reshape(count * 2, ncw)  32.4 us
    select_n x3, other arithmetic, shards(): cols = jnp.take(piece, col_index[slot], axis=3)  27.1 us
  transfers between devices with their start and end apart: 1, of which 1 were waited for; matrix products, arithmetic and copies ran while one was open for 0% of the time, Pallas kernels for 0%

commit v1 on v0

v1 whole, which is shorter than its diff:
```python
import functools

import jax
import jax.numpy as jnp
from jax import lax
from jax.experimental import pallas as pl
from jax.experimental.pallas import tpu as pltpu
from jax.sharding import PartitionSpec as P

MESH = pl.DeviceIdType.MESH
W = 32
G = 40
NX, NZ, NC, NY, NL = 4, 4, 2, 4, 2
NW = NY * NL
ROWS = 144
TILES = 54
XT = 14


def correlate(x_ref, m_ref, nat, rows_f, rows_s, cols_s, rr, gt, hb, other, sib, part, rsr,
              ss_r, rs_r, ss_h, rs_h, ss_g, rs_g, ss_w, rs_w, ss_c, rs_c, ss_x, rs_x,
              ss_z, rs_z, ss_a, rs_a, ss_s, rs_s):
    blk, w = lax.axis_index("blk"), lax.axis_index("walker")
    x, zh, c = blk // (NZ * NC), blk // NC % NZ, blk % NC
    y, zl = w // NL, w % NL

    def dev(x_=x, zh_=zh, c_=c, y_=y, zl_=zl):
        return ((x_ * NZ + zh_) * NC + c_, y_ * NL + zl_)

    def copy(src, dst, send, recv, to):
        return pltpu.make_async_remote_copy(
            src_ref=src, dst_ref=dst, send_sem=send, recv_sem=recv, device_id=to, device_id_type=MESH)

    x_peer = [None] + [lax.rem(x + d, NX) for d in (1, 2, 3)]
    x_from = [None] + [lax.rem(x + NX - d, NX) for d in (1, 2, 3)]
    z_peer = [None] + [lax.rem(zh + d, NZ) for d in (1, 2, 3)]
    z_from = [None] + [lax.rem(zh + NZ - d, NZ) for d in (1, 2, 3)]
    y_peer = [None] + [lax.rem(y + d, NY) for d in (1, 2, 3)]
    y_from = [None] + [lax.rem(y + NY - d, NY) for d in (1, 2, 3)]
    co, lo = 1 - c, 1 - zl
    sibling = dev(c_=co)
    sends = []

    def start(copy_):
        copy_.start()
        sends.append(copy_)

    barrier = pltpu.get_barrier_semaphore()
    peers = [sibling] + [dev(x_=x_peer[d]) for d in (1, 2, 3)] + [dev(zh_=z_peer[d]) for d in (1, 2, 3)]
    w_peer = [None] + [lax.rem(w + d, NW) for d in range(1, NW)]
    w_from = [None] + [lax.rem(w + NW - d, NW) for d in range(1, NW)]
    peers += [(blk, w_peer[d]) for d in range(1, NW)]
    for to in peers:
        pl.semaphore_signal(barrier, inc=1, device_id=to, device_id_type=MESH)

    with jax.named_scope("prep"):
        for i in range(8):
            pair = x_ref[i // 2, i % 2].astype(jnp.float32)
            nat[i:i + 1, :] = pair[0:1]
            nat[i + 8:i + 9, :] = pair[1:2]
        zeros = jnp.zeros((16, 8), jnp.float32)
        for t in range(12):
            tile = jnp.concatenate([nat[:, 120 * t:120 * t + 120], zeros], axis=1)
            cols_s[t // 3, :, 128 * (t % 3):128 * (t % 3) + 128] = tile.astype(jnp.bfloat16)
        for v in range(NW):
            first = 9 * (v // 2) + (5 if v % 2 else 0)
            half = 9 * (v // 2) + 4
            for i in range(4):
                rows_f[:, 32 * i:32 * i + 32] = nat[:, G * (first + i):G * (first + i) + W]
            lane = G * half + 16 * (v % 2)
            rows_f[:, 128:144] = nat[:, lane:lane + 16]
            rows_s[v] = rows_f[...].astype(jnp.bfloat16)

    with jax.named_scope("barrier"):
        pl.semaphore_wait(barrier, len(peers))

    for d in (2, 1, 3):
        start(copy(cols_s.at[z_peer[d]], hb.at[w, zh], ss_h.at[d], rs_h.at[d], dev(zh_=z_peer[d])))
    for d in range(1, NW):
        start(copy(rows_s.at[w_peer[d]], rr.at[w], ss_r.at[d], rs_r.at[d], (blk, w_peer[d])))
    rr[w] = rows_s[w]
    hb[w, zh] = cols_s[zh]

    with jax.named_scope("wait_h"):
        for d in (1, 3, 2):
            slot = hb.at[w, z_from[d]]
            copy(slot, slot, ss_h.at[d], rs_h.at[d], dev(zh_=z_from[d])).wait_recv()
    start(copy(hb.at[w], hb.at[w], ss_w.at[0], rs_w.at[0], dev(zl_=lo)))
    for d in (2, 1, 3):
        start(copy(hb.at[w], hb.at[w], ss_w.at[d], rs_w.at[d], dev(y_=y_peer[d])))

    with jax.named_scope("wait_r"):
        for d in range(1, NW):
            slot = rr.at[w_from[d]]
            copy(slot, slot, ss_r.at[d], rs_r.at[d], (blk, w_from[d])).wait_recv()
    with jax.named_scope("transpose"):
        turned = rr[...].reshape(NW * 16, 256).astype(jnp.float32).T.astype(jnp.bfloat16)
        whole = pl.multiple_of(16 * zl, 16)
        shared = pl.multiple_of(128 * (1 - zl), 16)
        gt[zh, pl.ds(whole, 128), :] = turned[0:128]
        gt[zh, pl.ds(shared, 16), :] = turned[128:144]
    for d in (2, 1, 3):
        start(copy(gt.at[zh], gt.at[zh], ss_g.at[d], rs_g.at[d], dev(zh_=z_peer[d])))

    with jax.named_scope("wait_w0"):
        slot = hb.at[y * NL + lo]
        copy(slot, slot, ss_w.at[0], rs_w.at[0], dev(zl_=lo)).wait_recv()
    for d in (2, 1, 3):
        start(copy(slot, slot, ss_w.at[3 + d], rs_w.at[3 + d], dev(y_=y_peer[d])))

    with jax.named_scope("wait_g"):
        for d in (1, 3, 2):
            slot = gt.at[z_from[d]]
            copy(slot, slot, ss_g.at[d], rs_g.at[d], dev(zh_=z_from[d])).wait_recv()
    left = jnp.concatenate([gt[i] for i in range(NZ)], axis=1).astype(jnp.float32)
    lane = lax.broadcasted_iota(jnp.int32, (ROWS, NZ * 128), 1)
    real = lane % 16 < 8
    left_re = jnp.where(real, left, -left)
    left_im = jnp.where(real, pltpu.roll(left, NZ * 128 - 8, 1), pltpu.roll(left, 8, 1))
    is_re = c == 0
    mine = jnp.where(is_re, left_re, left_im).astype(jnp.bfloat16)
    theirs = jnp.where(is_re, left_im, left_re).astype(jnp.bfloat16)

    with jax.named_scope("wait_w"):
        for d in (1, 3, 2):
            for add, l in ((0, zl), (3, lo)):
                slot = hb.at[y_from[d] * NL + l]
                copy(slot, slot, ss_w.at[add + d], rs_w.at[add + d], dev(y_=y_from[d])).wait_recv()
    with jax.named_scope("dots"):
        right = jnp.concatenate([hb[v, i] for i in range(NZ) for v in range(NW)], axis=0)
        product = jnp.dot(theirs, right, preferred_element_type=jnp.float32)
        for l in range(3):
            other[18 * l:18 * l + 18] = product[:, 128 * l:128 * l + 128].reshape(18, 8, 128)
        other[TILES:] = jnp.zeros((4 * XT - TILES, 8, 128), jnp.float32)
        order = [x_peer[2], x_peer[1], x_peer[3], x]
        for i, at in enumerate(order):
            start(copy(other.at[pl.ds(at * XT, XT)], sib.at[pl.ds(at * XT, XT)], ss_c.at[i], rs_c.at[i], sibling))
        product = jnp.dot(mine, right, preferred_element_type=jnp.float32)
        for l in range(3):
            part[18 * l:18 * l + 18] = product[:, 128 * l:128 * l + 128].reshape(18, 8, 128)
        part[TILES:] = jnp.zeros((4 * XT - TILES, 8, 128), jnp.float32)

    with jax.named_scope("core_sum"):
        for i, (at, d) in enumerate(zip(order, (2, 1, 3, 0))):
            here = pl.ds(at * XT, XT)
            slot = sib.at[here]
            copy(slot, slot, ss_c.at[i], rs_c.at[i], sibling).wait_recv()
            part[here] = part[here] + sib[here]
            if d:
                start(copy(part.at[here], rsr.at[d], ss_x.at[d], rs_x.at[d], dev(x_=at)))
    with jax.named_scope("x_sum"):
        total = part[pl.ds(x * XT, XT)]
        for d in (1, 3, 2):
            copy(rsr.at[d], rsr.at[d], ss_x.at[d], rs_x.at[d], dev(x_=x_from[d])).wait_recv()
            total = total + rsr[d]
        m_ref[c, zh, x] = total * ((2.0 * 1024) ** -0.5)

    def spread(n, zh_):
        slot = m_ref.at[c, zh_, x]
        for d in (2, 1, 3):
            start(copy(slot, slot, ss_a.at[3 * n + d - 1], rs_a.at[3 * n + d - 1], dev(x_=x_peer[d])))
        start(copy(slot, slot, ss_s.at[4 * n], rs_s.at[4 * n], sibling))

    slot = m_ref.at[c, zh, x]
    for d in (2, 1, 3):
        start(copy(slot, slot, ss_z.at[d], rs_z.at[d], dev(zh_=z_peer[d])))
    spread(0, zh)
    with jax.named_scope("z_gather"):
        for d in (1, 3, 2):
            slot = m_ref.at[c, z_from[d], x]
            copy(slot, slot, ss_z.at[d], rs_z.at[d], dev(zh_=z_from[d])).wait_recv()
            spread(d, z_from[d])
    with jax.named_scope("x_gather"):
        for n in (0, 1, 3, 2):
            for d in (1, 3, 2):
                at = zh if n == 0 else z_from[n]
                slot = m_ref.at[c, at, x_from[d]]
                copy(slot, slot, ss_a.at[3 * n + d - 1], rs_a.at[3 * n + d - 1], dev(x_=x_from[d])).wait_recv()
                start(copy(slot, slot, ss_s.at[4 * n + d], rs_s.at[4 * n + d], sibling))
    with jax.named_scope("core_gather"):
        for n in range(4):
            for d in range(4):
                slot = m_ref.at[co, zh if n == 0 else z_from[n], x if d == 0 else x_from[d]]
                copy(slot, slot, ss_s.at[4 * n + d], rs_s.at[4 * n + d], sibling).wait_recv()
    with jax.named_scope("sends"):
        for copy_ in sends:
            copy_.wait_send()


def correlation(measured):
    sem = lambda n: pltpu.SemaphoreType.DMA((n,))
    return pl.pallas_call(
        correlate,
        out_shape=jax.ShapeDtypeStruct((NC, NZ, NX, XT, 8, 128), jnp.float32),
        in_specs=[pl.BlockSpec(memory_space=pltpu.VMEM)],
        out_specs=pl.BlockSpec(memory_space=pltpu.VMEM),
        scratch_shapes=[
            pltpu.VMEM((16, 1440), jnp.float32),
            pltpu.VMEM((16, 256), jnp.float32),
            pltpu.VMEM((NW, 16, 256), jnp.bfloat16),
            pltpu.VMEM((NZ, 16, 384), jnp.bfloat16),
            pltpu.VMEM((NW, 16, 256), jnp.bfloat16),
            pltpu.VMEM((NZ, ROWS, 128), jnp.bfloat16),
            pltpu.VMEM((NW, NZ, 16, 384), jnp.bfloat16),
            pltpu.VMEM((4 * XT, 8, 128), jnp.float32),
            pltpu.VMEM((4 * XT, 8, 128), jnp.float32),
            pltpu.VMEM((4 * XT, 8, 128), jnp.float32),
            pltpu.VMEM((NX, XT, 8, 128), jnp.float32),
            sem(NW), sem(NW), sem(NZ), sem(NZ), sem(NZ), sem(NZ), sem(7), sem(7), sem(4), sem(4),
            sem(NX), sem(NX), sem(NZ), sem(NZ), sem(12), sem(12), sem(16), sem(16),
        ],
        compiler_params=pltpu.CompilerParams(
            collective_id=0, has_side_effects=True, vmem_limit_bytes=16 << 20),
    )(measured)


def select(per_dev, q_ref, nu_ref, kq_ref, m_ref, o_ref):
    base = lax.axis_index("blk") * per_dev
    lane = lax.broadcasted_iota(jnp.int32, (18, 8, 128), 2)

    def column_tile(tile, carry):
        for s in range(per_dev):
            q, nu = q_ref[base + s], nu_ref[base + s]
            parts = [[], []]
            for j in range(4):
                k = kq_ref[tile * 4 + j, q]
                shift = lax.rem(32 * j + 256 - (k % 3) * G - nu, 128)
                for part in range(2):
                    block = m_ref[part, k // 9, pl.ds(k % 9 // 3 * 18, 18)]
                    parts[part].append(pltpu.roll(block, shift, 2))
            for part in range(2):
                a, b, e, f = parts[part]
                row = jnp.where(lane < 64, jnp.where(lane < 32, a, b), jnp.where(lane < 96, e, f))
                o_ref[:, s, part, pl.ds(pl.multiple_of(tile * 128, 128), 128)] = row.reshape(ROWS, 128)
        return carry

    lax.fori_loop(0, 9, column_tile, 0)


def shards(measured, slice_q, slice_nu, kplusq):
    per_dev = slice_q.shape[0] // lax.axis_size("blk")
    m = correlation(measured).reshape(NC, NZ, NX * XT, 8, 128)
    smem, vmem = pl.BlockSpec(memory_space=pltpu.SMEM), pl.BlockSpec(memory_space=pltpu.VMEM)
    return pl.pallas_call(
        functools.partial(select, per_dev),
        out_shape=jax.ShapeDtypeStruct((ROWS, per_dev, 2, 36 * W), jnp.float32),
        in_specs=[smem, smem, smem, vmem],
        out_specs=vmem,
        compiler_params=pltpu.CompilerParams(vmem_limit_bytes=16 << 20),
    )(slice_q, slice_nu, kplusq, m)


def solution(mesh):
    return jax.shard_map(
        shards,
        mesh=mesh,
        in_specs=(P(("blk", "walker"), None, None, None), P(), P(), P()),
        out_specs=P("walker", "blk", None, None),
        check_vma=False,
    )
```

time: 1140 us -> 57.6 us (0.05); the launches traced: 1130 us -> 57.4 us
  waiting for transfers between devices: 729 us -> 0 us
  local copies, waits for them, and re-layouts: 300 us -> 2.83 us
  Pallas kernels: 0 us -> 54.5 us
  other arithmetic: 42.6 us -> 0 us
  matrix products: 40.6 us -> 0 us
  between operations: 13.8 us -> 0.02 us
    all_gather x1 -> x0, waiting for transfers between devices: 728 us -> none  [shards(): piece = lax.all_gather(measured, ('blk', 'walker'), axis=0, tiled=True)]
    gather x6 -> x0, local copies, waits for them, and re-layouts: 106 us -> none  [the longest x2 87.1 us: shards(): cols = jnp.take(piece, col_index[slot], axis=3)]
    slice x10 -> x0, local copies, waits for them, and re-layouts: 86.3 us -> none  [the longest x4 47.6 us: shards(): product_imaginary = cols[:, :, 1].reshape(count * 2, ncw)]
    all_gather x1 -> x0, local copies, waits for them, and re-layouts: 57.5 us -> none  [shards(): piece = lax.all_gather(measured, ('blk', 'walker'), axis=0, tiled=True)]
    pallas_call x0 -> x2, Pallas kernels: none -> 54.5 us  [the longest x1 47.9 us: correlation(): pl.pallas_call(correlate, out_shape=jax.ShapeDtypeStruct((NC, NZ, NX, XT,...]
    another operation x8 -> x0, local copies, waits for them, and re-layouts: 48.1 us -> none  [the longest x2 21.7 us: shards(): product_imaginary = cols[:, :, 1].reshape(count * 2, ncw)]
    dot_general x2 -> x0, matrix products: 40.6 us -> none  [shards(): jnp.einsum('kr,kc->rc', left_factor, right, preferred_element_type=jnp.fl...]
    select_n x8 -> x0, other arithmetic: 28.4 us -> none  [the longest x3 27.1 us: shards(): cols = jnp.take(piece, col_index[slot], axis=3)]
  transfers between devices with their start and end apart: 1 -> 0, of which waited for: 1 -> 0; matrix products, arithmetic and copies ran while one was open for 0% -> 0% of each run, Pallas kernels for 0% -> 0%
where the time goes in v1:
time: 57.6 us; the launch traced here: 57.4 us
  Pallas kernels  54.5 us (95%)
  local copies, waits for them, and re-layouts  2.83 us (5%)
    pallas_call x1, Pallas kernels, correlation(): pl.pallas_call(correlate, out_shape=jax.ShapeDtypeStruct((NC, NZ, NX, XT,...  47.9 us
    pallas_call x1, Pallas kernels, shards(): pl.pallas_call(functools.partial(select, per_dev), out_shape=jax.ShapeDty...  6.67 us
    unnamed x8, local copies, waits for them, and re-layouts  2.83 us

profile of v1, /device:TPU:1, one launch (start us, length us, event | category | flops | bytes accessed | tf_op | source)
XLA Modules:
  0.0 57.4 jit_solution(3288470234801585054)
XLA Ops:
  0.0 0.0 copy-start
  0.0 0.8 %copy-done = bf16[4,2,2,1440]{3,2,1,0:T(2,128)(2,1)S(1)} copy-done((bf16[4,2,2,1440]{3,2,1,0:T(2,128)(2,1)S(1)}, bf16[4,2,2,1440]{3,2,1,0:T(2,128)(2,1)}, u32[]{:S(2)}) %copy-start) | copy-done | bytes 46104
  0.8 47.9 %shard_map.46 = f32[2,4,4,14,8,128]{5,4,3,2,1,0:T(8,128)S(1)} custom-call(bf16[4,2,2,1440]{3,2,1,0:T(2,128)(2,1)S(1)} %copy-done), custom_call_target="tpu_custom_call" | custom-call | tf_op jit(solution)/shard_map/pallas_call | solution.py:192
  48.7 0.0 copy-start.1
  48.7 0.7 %copy-done.1 = s32[36,36]{1,0:T(8,128)S(1)} copy-done((s32[36,36]{1,0:T(8,128)S(1)}, s32[36,36]{1,0:T(8,128)}, u32[]{:S(2)}) %copy-start.1) | copy-done | bytes 5208
  49.4 0.0 copy-start.2
  49.4 0.7 %copy-done.2 = s32[64]{0:T(128)S(1)} copy-done((s32[64]{0:T(128)S(1)}, s32[64]{0:T(128)}, u32[]{:S(2)}) %copy-start.2) | copy-done | bytes 280
  50.1 0.0 copy-start.3
  50.1 0.7 %copy-done.3 = s32[64]{0:T(128)S(1)} copy-done((s32[64]{0:T(128)S(1)}, s32[64]{0:T(128)}, u32[]{:S(2)}) %copy-start.3) | copy-done | bytes 280
  50.7 6.7 %shard_map.47 = f32[144,2,2,1152]{3,2,1,0:T(2,128)} custom-call(s32[64]{0:T(128)S(1)} %copy-done.2, s32[64]{0:T(128)S(1)} %copy-done.3, s32[36,36]{1,0:T(8,128)S(1)} %copy-done.1, f32[2,4,56,8,128]{4,3,2,1,0:T(8,128)S(1)} %bitcast.1), custom_call_target="tpu_custom_call" | custom-call | tf_op jit(solution)/shard_map/pallas_call | solution.py:244
Async XLA Ops:
  0.0 0.8 %copy-start = (bf16[4,2,2,1440]{3,2,1,0:T(2,128)(2,1)S(1)}, bf16[4,2,2,1440]{3,2,1,0:T(2,128)(2,1)}, u32[]{:S(2)}) copy-start(bf16[4,2,2,1440]{3,2,1,0:T(2,128)(2,1)} %x_ref.1) | copy-start | bytes 138244
  48.7 0.7 %copy-start.1 = (s32[36,36]{1,0:T(8,128)S(1)}, s32[36,36]{1,0:T(8,128)}, u32[]{:S(2)}) copy-start(s32[36,36]{1,0:T(8,128)} %kq_ref.1) | copy-start | bytes 15556
  49.4 0.7 %copy-start.2 = (s32[64]{0:T(128)S(1)}, s32[64]{0:T(128)}, u32[]{:S(2)}) copy-start(s32[64]{0:T(128)} %q_ref.1) | copy-start | bytes 772
  50.1 0.7 %copy-start.3 = (s32[64]{0:T(128)S(1)}, s32[64]{0:T(128)}, u32[]{:S(2)}) copy-start(s32[64]{0:T(128)} %nu_ref.1) | copy-start | bytes 772

commit v2 on v0

v2 whole, which is shorter than its diff:
```python
import functools

import jax
import jax.numpy as jnp
from jax import lax
from jax.experimental import pallas as pl
from jax.experimental.pallas import tpu as pltpu
from jax.sharding import PartitionSpec as P

MESH = pl.DeviceIdType.MESH
W = 32
G = 40
NX, NZ, NC, NY, NL = 4, 4, 2, 4, 2
NW = NY * NL
ROWS = 144
TILES = 54
XT = 14
HT = XT // 2 + 1
LN2 = 0.6931471805599453


def encode(values):
    most = jnp.maximum(jnp.max(jnp.abs(values), axis=0), 1e-30)
    power = jnp.floor(jnp.log(most) * (1.0 / LN2)) + 1.0
    scaled = jnp.round(values * jnp.exp((15.0 - power) * LN2)[None])
    scaled = jnp.minimum(jnp.maximum(scaled, -32767.0), 32767.0).reshape(XT // 2, 16, 128)
    powers = jnp.concatenate([power, jnp.zeros_like(power)], axis=0)[None]
    return jnp.concatenate([scaled, powers], axis=0).astype(jnp.int32).astype(jnp.int16)


def decode(coded):
    values = coded.astype(jnp.int32).astype(jnp.float32)
    step = jnp.exp((values[XT // 2, 0:8] - 15.0) * LN2)
    return values[:XT // 2].reshape(XT, 8, 128) * step[None]


def correlate(x_hbm, m_hbm, x_ref, nat, rows_f, rows_s, cols_s, rr, gt, hb, other, sib, part, rsr, mq, ss_l, ss_r, rs_r,
              ss_h, rs_h, ss_g, rs_g, ss_w, rs_w, ss_c, rs_c, ss_x, rs_x, ss_z, rs_z, ss_a, rs_a, ss_s, rs_s, ss_o):
    blk, w = lax.axis_index("blk"), lax.axis_index("walker")
    x, zh, c = blk // (NZ * NC), blk // NC % NZ, blk % NC
    y, zl = w // NL, w % NL
    z = zh * NL + zl

    def dev(x_=x, zh_=zh, c_=c, y_=y, zl_=zl):
        return ((x_ * NZ + zh_) * NC + c_, y_ * NL + zl_)

    def copy(src, dst, send, recv, to):
        return pltpu.make_async_remote_copy(
            src_ref=src, dst_ref=dst, send_sem=send, recv_sem=recv, device_id=to, device_id_type=MESH)

    def ring(at, n):
        return ([at] + [lax.rem(at + d, n) for d in range(1, n)], [at] + [lax.rem(at + n - d, n) for d in range(1, n)])

    x_peer, x_from = ring(x, NX)
    zh_peer, zh_from = ring(zh, NZ)
    y_peer, y_from = ring(y, NY)
    z_peer, z_from = ring(z, NZ * NL)
    w_peer, w_from = ring(w, NW)
    co = 1 - c
    sibling = dev(c_=co)
    sends = []

    def start(copy_):
        copy_.start()
        sends.append(copy_)

    load = pltpu.make_async_copy(x_hbm, x_ref, ss_l.at[0])
    load.start()

    barrier = pltpu.get_barrier_semaphore()
    peers = [dev(zh_=z_peer[d] // NL, zl_=z_peer[d] % NL) for d in (4, 3, 5, 2, 6, 1, 7)]
    peers += [(blk, w_peer[d]) for d in range(1, NW)]
    peers += [dev(x_=x_peer[d]) for d in (1, 2, 3)] + [sibling]
    for to in peers:
        pl.semaphore_signal(barrier, inc=1, device_id=to, device_id_type=MESH)

    load.wait()
    for i in range(8):
        pair = x_ref[i // 2, i % 2].astype(jnp.float32)
        nat[i:i + 1, :] = pair[0:1]
        nat[i + 8:i + 9, :] = pair[1:2]
    for v in range(NW):
        first = 9 * (v // 2) + (5 if v % 2 else 0)
        half = 9 * (v // 2) + 4
        for i in range(4):
            rows_f[:, 32 * i:32 * i + 32] = nat[:, G * (first + i):G * (first + i) + W]
        lane = G * half + 16 * (v % 2)
        rows_f[:, 128:144] = nat[:, lane:lane + 16]
        rows_s[v] = rows_f[...].astype(jnp.bfloat16)
    zeros = jnp.zeros((16, 8), jnp.float32)
    for t in range(12):
        tile = jnp.concatenate([nat[:, 120 * t:120 * t + 120], zeros], axis=1)
        cols_s[t // 3, :, 128 * (t % 3):128 * (t % 3) + 128] = tile.astype(jnp.bfloat16)

    pl.semaphore_wait(barrier, len(peers))

    for d in range(1, NW):
        start(copy(rows_s.at[w_peer[d]], rr.at[w], ss_r.at[d], rs_r.at[d], (blk, w_peer[d])))
    for d in (4, 3, 5, 2, 6, 1, 7):
        to = z_peer[d]
        start(copy(cols_s.at[to // NL], hb.at[y, z], ss_h.at[d], rs_h.at[d], dev(zh_=to // NL, zl_=to % NL)))
    rr[w] = rows_s[w]
    hb[y, z] = cols_s[zh]

    def along_y(n):
        slot = hb.at[y, z_from[n]]
        for d in (2, 1, 3):
            start(copy(slot, slot, ss_w.at[4 * n + d], rs_w.at[4 * n + d], dev(y_=y_peer[d])))

    along_y(0)

    def arrived_h(n):
        slot = hb.at[y, z_from[n]]
        copy(slot, slot, ss_h.at[n], rs_h.at[n], dev(zh_=z_from[n] // NL, zl_=z_from[n] % NL)).wait_recv()
        along_y(n)

    for n in (1, 7, 2, 6):
        arrived_h(n)
    for d in range(1, NW):
        slot = rr.at[w_from[d]]
        copy(slot, slot, ss_r.at[d], rs_r.at[d], (blk, w_from[d])).wait_recv()
    turned = rr[...].reshape(NW * 16, 256).astype(jnp.float32).T.astype(jnp.bfloat16)
    whole = pl.multiple_of(16 * zl, 16)
    shared = pl.multiple_of(128 * (1 - zl), 16)
    gt[zh, pl.ds(whole, 128), :] = turned[0:128]
    gt[zh, pl.ds(shared, 16), :] = turned[128:144]
    for d in (2, 1, 3):
        start(copy(gt.at[zh], gt.at[zh], ss_g.at[d], rs_g.at[d], dev(zh_=zh_peer[d])))
    for n in (3, 5, 4):
        arrived_h(n)

    for n in (0, 1, 7, 2, 6, 3, 5, 4):
        for d in (1, 3, 2):
            slot = hb.at[y_from[d], z_from[n]]
            copy(slot, slot, ss_w.at[4 * n + d], rs_w.at[4 * n + d], dev(y_=y_from[d])).wait_recv()
    for d in (1, 3, 2):
        slot = gt.at[zh_from[d]]
        copy(slot, slot, ss_g.at[d], rs_g.at[d], dev(zh_=zh_from[d])).wait_recv()
    left = jnp.concatenate([gt[i] for i in range(NZ)], axis=1).astype(jnp.float32)
    lane = lax.broadcasted_iota(jnp.int32, (ROWS, NZ * 128), 1)
    real = lane % 16 < 8
    left_re = jnp.where(real, left, -left)
    left_im = jnp.where(real, pltpu.roll(left, NZ * 128 - 8, 1), pltpu.roll(left, 8, 1))
    is_re = c == 0
    mine = jnp.where(is_re, left_re, left_im).astype(jnp.bfloat16)
    theirs = jnp.where(is_re, left_im, left_re).astype(jnp.bfloat16)
    right = jnp.concatenate([hb[v // NL, i * NL + v % NL] for i in range(NZ) for v in range(NW)], axis=0)
    product = jnp.dot(theirs, right, preferred_element_type=jnp.float32)
    for l in range(3):
        other[18 * l:18 * l + 18] = product[:, 128 * l:128 * l + 128].reshape(18, 8, 128)
    other[TILES:] = jnp.zeros((4 * XT - TILES, 8, 128), jnp.float32)
    order = [x_peer[2], x_peer[1], x_peer[3], x]
    for i, at in enumerate(order):
        start(copy(other.at[pl.ds(at * XT, XT)], sib.at[pl.ds(at * XT, XT)], ss_c.at[i], rs_c.at[i], sibling))
    product = jnp.dot(mine, right, preferred_element_type=jnp.float32)
    for l in range(3):
        part[18 * l:18 * l + 18] = product[:, 128 * l:128 * l + 128].reshape(18, 8, 128)
    part[TILES:] = jnp.zeros((4 * XT - TILES, 8, 128), jnp.float32)

    for i, (at, d) in enumerate(zip(order, (2, 1, 3, 0))):
        here = pl.ds(at * XT, XT)
        slot = sib.at[here]
        copy(slot, slot, ss_c.at[i], rs_c.at[i], sibling).wait_recv()
        part[here] = part[here] + sib[here]
        if d:
            start(copy(part.at[here], rsr.at[d], ss_x.at[d], rs_x.at[d], dev(x_=at)))
    total = part[pl.ds(x * XT, XT)]
    for d in (1, 3, 2):
        copy(rsr.at[d], rsr.at[d], ss_x.at[d], rs_x.at[d], dev(x_=x_from[d])).wait_recv()
        total = total + rsr[d]
    mq[zh, x] = encode(total * ((2.0 * 1024) ** -0.5))

    keeps = []

    def arrived(n, d):
        at, slot = (zh_from[n], x_from[d]), mq.at[zh_from[n], x_from[d]]
        start(copy(slot, m_hbm.at[(c, *at)], ss_s.at[4 * n + d], rs_s.at[4 * n + d], sibling))
        keeps.append(pltpu.make_async_copy(slot, m_hbm.at[(c, *at)], ss_o.at[4 * n + d]))
        keeps[-1].start()

    def spread(n):
        slot = mq.at[zh_from[n], x]
        for d in (2, 1, 3):
            start(copy(slot, slot, ss_a.at[4 * n + d], rs_a.at[4 * n + d], dev(x_=x_peer[d])))
        arrived(n, 0)

    slot = mq.at[zh, x]
    for d in (2, 1, 3):
        start(copy(slot, slot, ss_z.at[d], rs_z.at[d], dev(zh_=zh_peer[d])))
    spread(0)
    for n in (1, 3, 2):
        slot = mq.at[zh_from[n], x]
        copy(slot, slot, ss_z.at[n], rs_z.at[n], dev(zh_=zh_from[n])).wait_recv()
        spread(n)
    for n in (0, 1, 3, 2):
        for d in (1, 3, 2):
            slot = mq.at[zh_from[n], x_from[d]]
            copy(slot, slot, ss_a.at[4 * n + d], rs_a.at[4 * n + d], dev(x_=x_from[d])).wait_recv()
            arrived(n, d)
    for copy_ in keeps:
        copy_.wait()
    for n in range(NZ):
        for d in range(NX):
            slot = m_hbm.at[co, zh_from[n], x_from[d]]
            copy(slot, slot, ss_s.at[4 * n + d], rs_s.at[4 * n + d], sibling).wait_recv()
    for copy_ in sends:
        copy_.wait_send()


def correlation(measured):
    sem = lambda n: pltpu.SemaphoreType.DMA((n,))
    return pl.pallas_call(
        correlate,
        out_shape=jax.ShapeDtypeStruct((NC, NZ, NX, HT, 16, 128), jnp.int16),
        in_specs=[pl.BlockSpec(memory_space=pltpu.HBM)],
        out_specs=pl.BlockSpec(memory_space=pltpu.HBM),
        scratch_shapes=[
            pltpu.VMEM(measured.shape, jnp.bfloat16),
            pltpu.VMEM((16, 1440), jnp.float32),
            pltpu.VMEM((16, 256), jnp.float32),
            pltpu.VMEM((NW, 16, 256), jnp.bfloat16),
            pltpu.VMEM((NZ, 16, 384), jnp.bfloat16),
            pltpu.VMEM((NW, 16, 256), jnp.bfloat16),
            pltpu.VMEM((NZ, ROWS, 128), jnp.bfloat16),
            pltpu.VMEM((NY, NZ * NL, 16, 384), jnp.bfloat16),
            pltpu.VMEM((4 * XT, 8, 128), jnp.float32),
            pltpu.VMEM((4 * XT, 8, 128), jnp.float32),
            pltpu.VMEM((4 * XT, 8, 128), jnp.float32),
            pltpu.VMEM((NX, XT, 8, 128), jnp.float32),
            pltpu.VMEM((NZ, NX, HT, 16, 128), jnp.int16),
            sem(1), sem(NW), sem(NW), sem(8), sem(8), sem(NZ), sem(NZ), sem(32), sem(32), sem(4), sem(4),
            sem(NX), sem(NX), sem(NZ), sem(NZ), sem(16), sem(16), sem(16), sem(16), sem(16),
        ],
        compiler_params=pltpu.CompilerParams(
            collective_id=0, has_side_effects=True, vmem_limit_bytes=60 << 20),
    )(measured)


def select(per_dev, q_hbm, nu_hbm, kq_hbm, mq_hbm, o_hbm, q_ref, nu_ref, kq_ref, mq, m_ref, o_ref, ss_l, ss_m, ss_o):
    tables = [pltpu.make_async_copy(src, dst, ss_l.at[i])
              for i, (src, dst) in enumerate(((q_hbm, q_ref), (nu_hbm, nu_ref), (kq_hbm, kq_ref)))]
    blocks = [pltpu.make_async_copy(mq_hbm.at[ri, zh], mq.at[ri, zh], ss_m.at[ri * NZ + zh])
              for ri in range(2) for zh in range(NZ)]
    for copy_ in blocks + tables:
        copy_.start()
    for ri in range(2):
        for zh in range(NZ):
            blocks[ri * NZ + zh].wait()
            for x in range(NX):
                m_ref[ri, zh, x * XT:(x + 1) * XT] = decode(mq[ri, zh, x])
    for copy_ in tables:
        copy_.wait()

    base = lax.axis_index("blk") * per_dev
    lane = lax.broadcasted_iota(jnp.int32, (18, 8, 128), 2)

    def out(tile, s):
        lanes = pl.ds(pl.multiple_of(tile * 128, 128), 128)
        return pltpu.make_async_copy(o_ref.at[tile, s], o_hbm.at[:, s, :, lanes], ss_o.at[tile * per_dev + s])

    def column_tile(tile, carry):
        for s in range(per_dev):
            q, nu = q_ref[base + s], nu_ref[base + s]
            parts = [[], []]
            for j in range(4):
                k = kq_ref[tile * 4 + j, q]
                shift = lax.rem(32 * j + 256 - (k % 3) * G - nu, 128)
                for ri in range(2):
                    block = m_ref[ri, k // 9, pl.ds(k % 9 // 3 * 18, 18)]
                    parts[ri].append(pltpu.roll(block, shift, 2))
            for ri in range(2):
                a, b, e, f = parts[ri]
                row = jnp.where(lane < 64, jnp.where(lane < 32, a, b), jnp.where(lane < 96, e, f))
                o_ref[tile, s, :, ri, :] = row.reshape(ROWS, 128)
            out(tile, s).start()
        return carry

    lax.fori_loop(0, 9, column_tile, 0)
    for tile in range(9):
        for s in range(per_dev):
            out(tile, s).wait()


def shards(measured, slice_q, slice_nu, kplusq):
    per_dev = slice_q.shape[0] // lax.axis_size("blk")
    sem = lambda n: pltpu.SemaphoreType.DMA((n,))
    return pl.pallas_call(
        functools.partial(select, per_dev),
        out_shape=jax.ShapeDtypeStruct((ROWS, per_dev, 2, 36 * W), jnp.float32),
        in_specs=[pl.BlockSpec(memory_space=pltpu.HBM)] * 4,
        out_specs=pl.BlockSpec(memory_space=pltpu.HBM),
        scratch_shapes=[
            pltpu.SMEM(slice_q.shape, jnp.int32),
            pltpu.SMEM(slice_nu.shape, jnp.int32),
            pltpu.SMEM(kplusq.shape, jnp.int32),
            pltpu.VMEM((NC, NZ, NX, HT, 16, 128), jnp.int16),
            pltpu.VMEM((NC, NZ, NX * XT, 8, 128), jnp.float32),
            pltpu.VMEM((9, per_dev, ROWS, 2, 128), jnp.float32),
            sem(3), sem(NC * NZ), sem(9 * per_dev),
        ],
        compiler_params=pltpu.CompilerParams(vmem_limit_bytes=60 << 20),
    )(slice_q, slice_nu, kplusq, correlation(measured))


def solution(mesh):
    return jax.shard_map(
        shards,
        mesh=mesh,
        in_specs=(P(("blk", "walker"), None, None, None), P(), P(), P()),
        out_specs=P("walker", "blk", None, None),
        check_vma=False,
    )
```

time: 1140 us -> 47.4 us (0.04); the launches traced: 1130 us -> 47.2 us
  waiting for transfers between devices: 729 us -> 0 us
  local copies, waits for them, and re-layouts: 300 us -> 0 us
  Pallas kernels: 0 us -> 47.2 us
  other arithmetic: 42.6 us -> 0 us
  matrix products: 40.6 us -> 0 us
  between operations: 13.8 us -> 0.01 us
    all_gather x1 -> x0, waiting for transfers between devices: 728 us -> none  [shards(): piece = lax.all_gather(measured, ('blk', 'walker'), axis=0, tiled=True)]
    gather x6 -> x0, local copies, waits for them, and re-layouts: 106 us -> none  [the longest x2 87.1 us: shards(): cols = jnp.take(piece, col_index[slot], axis=3)]
    slice x10 -> x0, local copies, waits for them, and re-layouts: 86.3 us -> none  [the longest x4 47.6 us: shards(): product_imaginary = cols[:, :, 1].reshape(count * 2, ncw)]
    all_gather x1 -> x0, local copies, waits for them, and re-layouts: 57.5 us -> none  [shards(): piece = lax.all_gather(measured, ('blk', 'walker'), axis=0, tiled=True)]
    another operation x8 -> x0, local copies, waits for them, and re-layouts: 48.1 us -> none  [the longest x2 21.7 us: shards(): product_imaginary = cols[:, :, 1].reshape(count * 2, ncw)]
    pallas_call x0 -> x2, Pallas kernels: none -> 47.2 us  [the longest x1 40.7 us: correlation(): pl.pallas_call(correlate, out_shape=jax.ShapeDtypeStruct((NC, NZ, NX, HT,...]
    dot_general x2 -> x0, matrix products: 40.6 us -> none  [shards(): jnp.einsum('kr,kc->rc', left_factor, right, preferred_element_type=jnp.fl...]
    select_n x8 -> x0, other arithmetic: 28.4 us -> none  [the longest x3 27.1 us: shards(): cols = jnp.take(piece, col_index[slot], axis=3)]
  transfers between devices with their start and end apart: 1 -> 0, of which waited for: 1 -> 0; matrix products, arithmetic and copies ran while one was open for 0% -> 0% of each run, Pallas kernels for 0% -> 0%
where the time goes in v2:
time: 47.4 us; the launch traced here: 47.2 us
  Pallas kernels  47.2 us (100%)
    pallas_call x1, Pallas kernels, correlation(): pl.pallas_call(correlate, out_shape=jax.ShapeDtypeStruct((NC, NZ, NX, HT,...  40.7 us
    pallas_call x1, Pallas kernels, shards(): pl.pallas_call(functools.partial(select, per_dev), out_shape=jax.ShapeDty...  6.52 us

profile of v2, /device:TPU:1, one launch (start us, length us, event | category | flops | bytes accessed | tf_op | source)
XLA Modules:
  0.0 47.2 jit_solution(2398136383992065077)
XLA Ops:
  0.0 40.7 %shard_map.46.mq_hbm = s16[2,4,4,8,16,128]{5,4,3,2,1,0:T(8,128)(2,1)} custom-call(bf16[4,2,2,1440]{3,2,1,0:T(2,128)(2,1)} %x_hbm.1), custom_call_target="tpu_custom_call" | custom-call | tf_op jit(solution)/shard_map/pallas_call | solution.py:212
  40.7 6.5 %shard_map.47 = f32[144,2,2,1152]{3,2,1,0:T(2,128)} custom-call(s32[64]{0:T(128)} %q_hbm.1, s32[64]{0:T(128)} %nu_hbm.1, s32[36,36]{1,0:T(8,128)} %kq_hbm.1, s16[2,4,4,8,16,128]{5,4,3,2,1,0:T(8,128)(2,1)} %shard_map.46.mq_hbm), custom_call_target="tpu_custom_call" | custom-call | tf_op jit(solution)/shard_map/pallas_call | solution.py:287

commit v3 on v2

--- a/solution.py
+++ b/solution.py
@@ -34,7 +34,7 @@
     return values[:XT // 2].reshape(XT, 8, 128) * step[None]
 
 
-def correlate(x_hbm, m_hbm, x_ref, nat, rows_f, rows_s, cols_s, rr, gt, hb, other, sib, part, rsr, mq, ss_l, ss_r, rs_r,
+def correlate(x_hbm, m_hbm, x_ref, nat, rows_f, rows_s, cols_s, rr, gt, hb, other, sib, part, sent, rsr, mq, ss_l, ss_r, rs_r,
               ss_h, rs_h, ss_g, rs_g, ss_w, rs_w, ss_c, rs_c, ss_x, rs_x, ss_z, rs_z, ss_a, rs_a, ss_s, rs_s, ss_o):
     blk, w = lax.axis_index("blk"), lax.axis_index("walker")
     x, zh, c = blk // (NZ * NC), blk // NC % NZ, blk % NC
@@ -96,7 +96,7 @@
 
     for d in range(1, NW):
         start(copy(rows_s.at[w_peer[d]], rr.at[w], ss_r.at[d], rs_r.at[d], (blk, w_peer[d])))
-    for d in (4, 3, 5, 2, 6, 1, 7):
+    for d in (1, 7, 2, 6, 3, 5, 4):
         to = z_peer[d]
         start(copy(cols_s.at[to // NL], hb.at[y, z], ss_h.at[d], rs_h.at[d], dev(zh_=to // NL, zl_=to % NL)))
     rr[w] = rows_s[w]
@@ -161,13 +161,13 @@
         here = pl.ds(at * XT, XT)
         slot = sib.at[here]
         copy(slot, slot, ss_c.at[i], rs_c.at[i], sibling).wait_recv()
-        part[here] = part[here] + sib[here]
+        total = part[here] + sib[here]
         if d:
-            start(copy(part.at[here], rsr.at[d], ss_x.at[d], rs_x.at[d], dev(x_=at)))
-    total = part[pl.ds(x * XT, XT)]
+            sent[d] = encode(total)
+            start(copy(sent.at[d], rsr.at[d], ss_x.at[d], rs_x.at[d], dev(x_=at)))
     for d in (1, 3, 2):
         copy(rsr.at[d], rsr.at[d], ss_x.at[d], rs_x.at[d], dev(x_=x_from[d])).wait_recv()
-        total = total + rsr[d]
+        total = total + decode(rsr[d])
     mq[zh, x] = encode(total * ((2.0 * 1024) ** -0.5))
 
     keeps = []
@@ -185,7 +185,7 @@
         arrived(n, 0)
 
     slot = mq.at[zh, x]
-    for d in (2, 1, 3):
+    for d in (1, 3, 2):
         start(copy(slot, slot, ss_z.at[d], rs_z.at[d], dev(zh_=zh_peer[d])))
     spread(0)
     for n in (1, 3, 2):
@@ -226,7 +226,8 @@
             pltpu.VMEM((4 * XT, 8, 128), jnp.float32),
             pltpu.VMEM((4 * XT, 8, 128), jnp.float32),
             pltpu.VMEM((4 * XT, 8, 128), jnp.float32),
-            pltpu.VMEM((NX, XT, 8, 128), jnp.float32),
+            pltpu.VMEM((NX, HT, 16, 128), jnp.int16),
+            pltpu.VMEM((NX, HT, 16, 128), jnp.int16),
             pltpu.VMEM((NZ, NX, HT, 16, 128), jnp.int16),
             sem(1), sem(NW), sem(NW), sem(8), sem(8), sem(NZ), sem(NZ), sem(32), sem(32), sem(4), sem(4),
             sem(NX), sem(NX), sem(NZ), sem(NZ), sem(16), sem(16), sem(16), sem(16), sem(16),
@@ -275,7 +276,7 @@
             out(tile, s).start()
         return carry
 
-    lax.fori_loop(0, 9, column_tile, 0)
+    lax.fori_loop(0, 9, column_tile, 0, unroll=True)
     for tile in range(9):
         for s in range(per_dev):
             out(tile, s).wait()

time: 47.4 us -> 44 us (0.928)
  Pallas kernels: 47.2 us -> 43.7 us
    pallas_call x1, Pallas kernels: 40.7 us -> 38.2 us  [correlation(): pl.pallas_call(correlate, out_shape=jax.ShapeDtypeStruct((NC, NZ, NX, HT,...]
    pallas_call x1, Pallas kernels: 6.52 us -> 5.5 us  [shards(): pl.pallas_call(functools.partial(select, per_dev), out_shape=jax.ShapeDty...]
where the time goes in v3:
time: 44 us; the launch traced here: 43.8 us
  Pallas kernels  43.7 us (99%)
    pallas_call x1, Pallas kernels, correlation(): pl.pallas_call(correlate, out_shape=jax.ShapeDtypeStruct((NC, NZ, NX, HT,...  38.2 us
    pallas_call x1, Pallas kernels, shards(): pl.pallas_call(functools.partial(select, per_dev), out_shape=jax.ShapeDty...  5.5 us

profile of v3, /device:TPU:1, one launch (start us, length us, event | category | flops | bytes accessed | tf_op | source)
XLA Modules:
  0.0 43.8 jit_solution(17950844426251282543)
XLA Ops:
  0.0 38.2 %shard_map.46.mq_hbm = s16[2,4,4,8,16,128]{5,4,3,2,1,0:T(8,128)(2,1)} custom-call(bf16[4,2,2,1440]{3,2,1,0:T(2,128)(2,1)} %x_hbm.1), custom_call_target="tpu_custom_call" | custom-call | tf_op jit(solution)/shard_map/pallas_call | solution.py:212
  38.3 5.5 %shard_map.47 = f32[144,2,2,1152]{3,2,1,0:T(2,128)} custom-call(s32[64]{0:T(128)} %q_hbm.1, s32[64]{0:T(128)} %nu_hbm.1, s32[36,36]{1,0:T(8,128)} %kq_hbm.1, s16[2,4,4,8,16,128]{5,4,3,2,1,0:T(8,128)(2,1)} %shard_map.46.mq_hbm), custom_call_target="tpu_custom_call" | custom-call | tf_op jit(solution)/shard_map/pallas_call | solution.py:288

commit v4 on v3

--- a/solution.py
+++ b/solution.py
@@ -34,8 +34,8 @@
     return values[:XT // 2].reshape(XT, 8, 128) * step[None]
 
 
-def correlate(x_hbm, m_hbm, x_ref, nat, rows_f, rows_s, cols_s, rr, gt, hb, other, sib, part, sent, rsr, mq, ss_l, ss_r, rs_r,
-              ss_h, rs_h, ss_g, rs_g, ss_w, rs_w, ss_c, rs_c, ss_x, rs_x, ss_z, rs_z, ss_a, rs_a, ss_s, rs_s, ss_o):
+def correlate(x_hbm, m_hbm, x_ref, nat, rows_f, rows_s, cols_s, rr, gt, hb, other, part, sent, rsr, mq, ss_l, ss_r, rs_r,
+              ss_h, rs_h, ss_g, rs_g, ss_w, rs_w, ss_x, rs_x, ss_z, rs_z, ss_a, rs_a, ss_s, rs_s, ss_o):
     blk, w = lax.axis_index("blk"), lax.axis_index("walker")
     x, zh, c = blk // (NZ * NC), blk // NC % NZ, blk % NC
     y, zl = w // NL, w % NL
@@ -64,13 +64,18 @@
         copy_.start()
         sends.append(copy_)
 
+    def sent_all(since=0):
+        for copy_ in sends[since:]:
+            copy_.wait_send()
+        del sends[since:]
+
     load = pltpu.make_async_copy(x_hbm, x_ref, ss_l.at[0])
     load.start()
 
     barrier = pltpu.get_barrier_semaphore()
     peers = [dev(zh_=z_peer[d] // NL, zl_=z_peer[d] % NL) for d in (4, 3, 5, 2, 6, 1, 7)]
     peers += [(blk, w_peer[d]) for d in range(1, NW)]
-    peers += [dev(x_=x_peer[d]) for d in (1, 2, 3)] + [sibling]
+    peers += [dev(x_=x_peer[d], c_=c_) for d in (1, 2, 3) for c_ in (c, co)] + [sibling, dev(zh_=zh_peer[2], c_=co)]
     for to in peers:
         pl.semaphore_signal(barrier, inc=1, device_id=to, device_id_type=MESH)
 
@@ -145,66 +150,97 @@
     mine = jnp.where(is_re, left_re, left_im).astype(jnp.bfloat16)
     theirs = jnp.where(is_re, left_im, left_re).astype(jnp.bfloat16)
     right = jnp.concatenate([hb[v // NL, i * NL + v % NL] for i in range(NZ) for v in range(NW)], axis=0)
-    product = jnp.dot(theirs, right, preferred_element_type=jnp.float32)
-    for l in range(3):
-        other[18 * l:18 * l + 18] = product[:, 128 * l:128 * l + 128].reshape(18, 8, 128)
-    other[TILES:] = jnp.zeros((4 * XT - TILES, 8, 128), jnp.float32)
-    order = [x_peer[2], x_peer[1], x_peer[3], x]
-    for i, at in enumerate(order):
-        start(copy(other.at[pl.ds(at * XT, XT)], sib.at[pl.ds(at * XT, XT)], ss_c.at[i], rs_c.at[i], sibling))
-    product = jnp.dot(mine, right, preferred_element_type=jnp.float32)
-    for l in range(3):
-        part[18 * l:18 * l + 18] = product[:, 128 * l:128 * l + 128].reshape(18, 8, 128)
-    part[TILES:] = jnp.zeros((4 * XT - TILES, 8, 128), jnp.float32)
-
-    for i, (at, d) in enumerate(zip(order, (2, 1, 3, 0))):
-        here = pl.ds(at * XT, XT)
-        slot = sib.at[here]
-        copy(slot, slot, ss_c.at[i], rs_c.at[i], sibling).wait_recv()
-        total = part[here] + sib[here]
-        if d:
-            sent[d] = encode(total)
-            start(copy(sent.at[d], rsr.at[d], ss_x.at[d], rs_x.at[d], dev(x_=at)))
-    for d in (1, 3, 2):
-        copy(rsr.at[d], rsr.at[d], ss_x.at[d], rs_x.at[d], dev(x_=x_from[d])).wait_recv()
-        total = total + decode(rsr[d])
+
+    def tiles(left_, to):
+        product = jnp.dot(left_, right, preferred_element_type=jnp.float32)
+        for l in range(3):
+            to[18 * l:18 * l + 18] = product[:, 128 * l:128 * l + 128].reshape(18, 8, 128)
+        to[TILES:] = jnp.zeros((4 * XT - TILES, 8, 128), jnp.float32)
+
+    def term(n, part, d, to):
+        sent[n] = encode(part[pl.ds(x_peer[d] * XT, XT)])
+        start(copy(sent.at[n], rsr.at[n], ss_x.at[n], rs_x.at[n], to))
+
+    tiles(theirs, other)
+    for d in (2, 1, 3, 0):
+        term(4 + d, other, d, dev(x_=x_peer[d], c_=co))
+    tiles(mine, part)
+    for d in (2, 1, 3):
+        term(d, part, d, dev(x_=x_peer[d]))
+    total = part[pl.ds(x * XT, XT)]
+    for n in (4, 5, 7, 1, 3, 6, 2):
+        source = dev(x_=x_from[n % 4], c_=co if n >= 4 else c)
+        copy(rsr.at[n], rsr.at[n], ss_x.at[n], rs_x.at[n], source).wait_recv()
+        total = total + decode(rsr[n])
     mq[zh, x] = encode(total * ((2.0 * 1024) ** -0.5))
 
     keeps = []
 
     def arrived(n, d):
         at, slot = (zh_from[n], x_from[d]), mq.at[zh_from[n], x_from[d]]
-        start(copy(slot, m_hbm.at[(c, *at)], ss_s.at[4 * n + d], rs_s.at[4 * n + d], sibling))
+        if n != 2 or d == 0:
+            start(copy(slot, m_hbm.at[(c, *at)], ss_s.at[4 * n + d], rs_s.at[4 * n + d], sibling))
         keeps.append(pltpu.make_async_copy(slot, m_hbm.at[(c, *at)], ss_o.at[4 * n + d]))
         keeps[-1].start()
 
     def spread(n):
         slot = mq.at[zh_from[n], x]
-        for d in (2, 1, 3):
+        for d in (2, 1, 3) if n != 2 else (1, 3):
             start(copy(slot, slot, ss_a.at[4 * n + d], rs_a.at[4 * n + d], dev(x_=x_peer[d])))
+            if n == 2:
+                start(copy(slot, m_hbm.at[c, zh_from[n], x], ss_s.at[4 * n + d], rs_s.at[4 * n + d], dev(x_=x_peer[d], c_=co)))
         arrived(n, 0)
 
+    def from_z(n):
+        slot = mq.at[zh_from[n], x]
+        copy(slot, slot, ss_z.at[n], rs_z.at[n], dev(zh_=zh_from[n])).wait_recv()
+        spread(n)
+
+    def from_x(n, d):
+        slot = mq.at[zh_from[n], x_from[d]]
+        source = dev(x_=x_from[d]) if (n, d) != (2, 2) else dev(zh_=zh_from[2])
+        copy(slot, slot, ss_a.at[4 * n + d], rs_a.at[4 * n + d], source).wait_recv()
+        arrived(n, d)
+
+    def from_sibling(n, d):
+        slot = m_hbm.at[co, zh_from[n], x_from[d]]
+        copy(slot, slot, ss_s.at[4 * n + d], rs_s.at[4 * n + d], sibling).wait_recv()
+
+    def kept():
+        for copy_ in keeps:
+            copy_.wait()
+        del keeps[:]
+
+    earlier = len(sends)
     slot = mq.at[zh, x]
     for d in (1, 3, 2):
         start(copy(slot, slot, ss_z.at[d], rs_z.at[d], dev(zh_=zh_peer[d])))
     spread(0)
-    for n in (1, 3, 2):
-        slot = mq.at[zh_from[n], x]
-        copy(slot, slot, ss_z.at[n], rs_z.at[n], dev(zh_=zh_from[n])).wait_recv()
-        spread(n)
-    for n in (0, 1, 3, 2):
-        for d in (1, 3, 2):
-            slot = mq.at[zh_from[n], x_from[d]]
-            copy(slot, slot, ss_a.at[4 * n + d], rs_a.at[4 * n + d], dev(x_=x_from[d])).wait_recv()
-            arrived(n, d)
-    for copy_ in keeps:
-        copy_.wait()
-    for n in range(NZ):
-        for d in range(NX):
-            slot = m_hbm.at[co, zh_from[n], x_from[d]]
-            copy(slot, slot, ss_s.at[4 * n + d], rs_s.at[4 * n + d], sibling).wait_recv()
-    for copy_ in sends:
+    for copy_ in sends[:earlier]:
         copy_.wait_send()
+    del sends[:earlier]
+    from_z(1)
+    from_z(3)
+    from_x(0, 2)
+    slot = mq.at[zh, x_from[2]]
+    start(copy(slot, slot, ss_a.at[10], rs_a.at[10], dev(zh_=zh_peer[2])))
+    start(copy(slot, m_hbm.at[c, zh, x_from[2]], ss_s.at[10], rs_s.at[10], dev(zh_=zh_peer[2], c_=co)))
+    earlier = len(sends)
+    from_z(2)
+    from_x(0, 1)
+    from_x(0, 3)
+    for copy_ in sends[:earlier]:
+        copy_.wait_send()
+    del sends[:earlier]
+    kept()
+    for n, d in ((0, 0), (1, 0), (3, 0), (0, 2), (2, 0), (0, 1), (0, 3)):
+        from_sibling(n, d)
+    for n, d in ((1, 1), (1, 3), (1, 2), (3, 1), (3, 3), (3, 2), (2, 2), (2, 1), (2, 3)):
+        from_x(n, d)
+    sent_all()
+    kept()
+    for n, d in ((1, 1), (1, 3), (1, 2), (3, 1), (3, 3), (3, 2), (2, 2), (2, 1), (2, 3)):
+        from_sibling(n, d)
 
 
 def correlation(measured):
@@ -225,12 +261,11 @@
             pltpu.VMEM((NY, NZ * NL, 16, 384), jnp.bfloat16),
             pltpu.VMEM((4 * XT, 8, 128), jnp.float32),
             pltpu.VMEM((4 * XT, 8, 128), jnp.float32),
-            pltpu.VMEM((4 * XT, 8, 128), jnp.float32),
-            pltpu.VMEM((NX, HT, 16, 128), jnp.int16),
-            pltpu.VMEM((NX, HT, 16, 128), jnp.int16),
+            pltpu.VMEM((NC * NX, HT, 16, 128), jnp.int16),
+            pltpu.VMEM((NC * NX, HT, 16, 128), jnp.int16),
             pltpu.VMEM((NZ, NX, HT, 16, 128), jnp.int16),
-            sem(1), sem(NW), sem(NW), sem(8), sem(8), sem(NZ), sem(NZ), sem(32), sem(32), sem(4), sem(4),
-            sem(NX), sem(NX), sem(NZ), sem(NZ), sem(16), sem(16), sem(16), sem(16), sem(16),
+            sem(1), sem(NW), sem(NW), sem(8), sem(8), sem(NZ), sem(NZ), sem(32), sem(32),
+            sem(8), sem(8), sem(NZ), sem(NZ), sem(16), sem(16), sem(16), sem(16), sem(16),
         ],
         compiler_params=pltpu.CompilerParams(
             collective_id=0, has_side_effects=True, vmem_limit_bytes=60 << 20),

time: 44 us -> 42.8 us (0.973)
  Pallas kernels: 43.7 us -> 42.6 us
    pallas_call x1, Pallas kernels: 38.2 us -> 37.1 us  [correlation(): pl.pallas_call(correlate, out_shape=jax.ShapeDtypeStruct((NC, NZ, NX, HT,...]
where the time goes in v4:
time: 42.8 us; the launch traced here: 42.6 us
  Pallas kernels  42.6 us (100%)
    pallas_call x1, Pallas kernels, correlation(): pl.pallas_call(correlate, out_shape=jax.ShapeDtypeStruct((NC, NZ, NX, HT,...  37.1 us
    pallas_call x1, Pallas kernels, shards(): pl.pallas_call(functools.partial(select, per_dev), out_shape=jax.ShapeDty...  5.5 us

profile of v4, /device:TPU:1, one launch (start us, length us, event | category | flops | bytes accessed | tf_op | source)
XLA Modules:
  0.0 42.6 jit_solution(2319758962753099197)
XLA Ops:
  0.0 37.1 %shard_map.46.mq_hbm = s16[2,4,4,8,16,128]{5,4,3,2,1,0:T(8,128)(2,1)} custom-call(bf16[4,2,2,1440]{3,2,1,0:T(2,128)(2,1)} %x_hbm.1), custom_call_target="tpu_custom_call" | custom-call | tf_op jit(solution)/shard_map/pallas_call | solution.py:248
  37.1 5.5 %shard_map.47 = f32[144,2,2,1152]{3,2,1,0:T(2,128)} custom-call(s32[64]{0:T(128)} %q_hbm.1, s32[64]{0:T(128)} %nu_hbm.1, s32[36,36]{1,0:T(8,128)} %kq_hbm.1, s16[2,4,4,8,16,128]{5,4,3,2,1,0:T(8,128)(2,1)} %shard_map.46.mq_hbm), custom_call_target="tpu_custom_call" | custom-call | tf_op jit(solution)/shard_map/pallas_call | solution.py:323

commit v5 on v4

--- a/solution.py
+++ b/solution.py
@@ -17,12 +17,14 @@
 XT = 14
 HT = XT // 2 + 1
 LN2 = 0.6931471805599453
+FAR_POWER = 64.0
+FAR = 2.0 ** 64
 
 
 def encode(values):
-    most = jnp.maximum(jnp.max(jnp.abs(values), axis=0), 1e-30)
+    most = jnp.maximum(jnp.max(jnp.abs(values), axis=0), 1e-37)
     power = jnp.floor(jnp.log(most) * (1.0 / LN2)) + 1.0
-    scaled = jnp.round(values * jnp.exp((15.0 - power) * LN2)[None])
+    scaled = jnp.round(values * FAR * jnp.exp((15.0 - FAR_POWER - power) * LN2)[None])
     scaled = jnp.minimum(jnp.maximum(scaled, -32767.0), 32767.0).reshape(XT // 2, 16, 128)
     powers = jnp.concatenate([power, jnp.zeros_like(power)], axis=0)[None]
     return jnp.concatenate([scaled, powers], axis=0).astype(jnp.int32).astype(jnp.int16)
@@ -30,8 +32,8 @@
 
 def decode(coded):
     values = coded.astype(jnp.int32).astype(jnp.float32)
-    step = jnp.exp((values[XT // 2, 0:8] - 15.0) * LN2)
-    return values[:XT // 2].reshape(XT, 8, 128) * step[None]
+    step = jnp.exp((values[XT // 2, 0:8] - 15.0 + FAR_POWER) * LN2)
+    return values[:XT // 2].reshape(XT, 8, 128) * step[None] * (1.0 / FAR)
 
 
 def correlate(x_hbm, m_hbm, x_ref, nat, rows_f, rows_s, cols_s, rr, gt, hb, other, part, sent, rsr, mq, ss_l, ss_r, rs_r,
@@ -134,37 +136,38 @@
     for n in (3, 5, 4):
         arrived_h(n)
 
-    for n in (0, 1, 7, 2, 6, 3, 5, 4):
-        for d in (1, 3, 2):
-            slot = hb.at[y_from[d], z_from[n]]
-            copy(slot, slot, ss_w.at[4 * n + d], rs_w.at[4 * n + d], dev(y_=y_from[d])).wait_recv()
-    for d in (1, 3, 2):
-        slot = gt.at[zh_from[d]]
-        copy(slot, slot, ss_g.at[d], rs_g.at[d], dev(zh_=zh_from[d])).wait_recv()
-    left = jnp.concatenate([gt[i] for i in range(NZ)], axis=1).astype(jnp.float32)
-    lane = lax.broadcasted_iota(jnp.int32, (ROWS, NZ * 128), 1)
-    real = lane % 16 < 8
-    left_re = jnp.where(real, left, -left)
-    left_im = jnp.where(real, pltpu.roll(left, NZ * 128 - 8, 1), pltpu.roll(left, 8, 1))
+    def term(n, part_, d, to):
+        sent[n] = encode(part_[pl.ds(x_peer[d] * XT, XT)])
+        start(copy(sent.at[n], rsr.at[n], ss_x.at[n], rs_x.at[n], to))
+
+    def add(left_, right_, to, first):
+        product = jnp.dot(left_.astype(jnp.bfloat16), right_, preferred_element_type=jnp.float32)
+        for l in range(3):
+            tiles = product[:, 128 * l:128 * l + 128].reshape(18, 8, 128)
+            to[18 * l:18 * l + 18] = tiles if first else to[18 * l:18 * l + 18] + tiles
+
+    other[TILES:] = jnp.zeros((4 * XT - TILES, 8, 128), jnp.float32)
+    part[TILES:] = jnp.zeros((4 * XT - TILES, 8, 128), jnp.float32)
+    real = lax.broadcasted_iota(jnp.int32, (ROWS, 128), 1) % 16 < 8
     is_re = c == 0
-    mine = jnp.where(is_re, left_re, left_im).astype(jnp.bfloat16)
-    theirs = jnp.where(is_re, left_im, left_re).astype(jnp.bfloat16)
-    right = jnp.concatenate([hb[v // NL, i * NL + v % NL] for i in range(NZ) for v in range(NW)], axis=0)
-
-    def tiles(left_, to):
-        product = jnp.dot(left_, right, preferred_element_type=jnp.float32)
-        for l in range(3):
-            to[18 * l:18 * l + 18] = product[:, 128 * l:128 * l + 128].reshape(18, 8, 128)
-        to[TILES:] = jnp.zeros((4 * XT - TILES, 8, 128), jnp.float32)
-
-    def term(n, part, d, to):
-        sent[n] = encode(part[pl.ds(x_peer[d] * XT, XT)])
-        start(copy(sent.at[n], rsr.at[n], ss_x.at[n], rs_x.at[n], to))
-
-    tiles(theirs, other)
-    for d in (2, 1, 3, 0):
-        term(4 + d, other, d, dev(x_=x_peer[d], c_=co))
-    tiles(mine, part)
+    for n in (0, 1, 3, 2):
+        at = zh_from[n]
+        for l in range(NL):
+            apart = lax.rem(z - (at * NL + l) + 8, 8)
+            for d in (1, 3, 2):
+                slot = hb.at[y_from[d], at * NL + l]
+                copy(slot, slot, ss_w.at[4 * apart + d], rs_w.at[4 * apart + d], dev(y_=y_from[d])).wait_recv()
+        if n:
+            copy(gt.at[at], gt.at[at], ss_g.at[n], rs_g.at[n], dev(zh_=at)).wait_recv()
+        left = gt[at].astype(jnp.float32)
+        left_re = jnp.where(real, left, -left)
+        left_im = jnp.where(real, pltpu.roll(left, 120, 1), pltpu.roll(left, 8, 1))
+        right = jnp.concatenate([hb[v // NL, at * NL + v % NL] for v in range(NW)], axis=0)
+        add(jnp.where(is_re, left_im, left_re), right, other, n == 0)
+        if n == 2:
+            for d in (2, 1, 3, 0):
+                term(4 + d, other, d, dev(x_=x_peer[d], c_=co))
+        add(jnp.where(is_re, left_re, left_im), right, part, n == 0)
     for d in (2, 1, 3):
         term(d, part, d, dev(x_=x_peer[d]))
     total = part[pl.ds(x * XT, XT)]

time: 42.8 us -> 42.8 us (level)
  no operation moved by 1% of the time
where the time goes in v5:
time: 42.8 us; the launch traced here: 42.6 us
  Pallas kernels  42.6 us (100%)
    pallas_call x1, Pallas kernels, correlation(): pl.pallas_call(correlate, out_shape=jax.ShapeDtypeStruct((NC, NZ, NX, HT,...  37.1 us
    pallas_call x1, Pallas kernels, shards(): pl.pallas_call(functools.partial(select, per_dev), out_shape=jax.ShapeDty...  5.51 us

profile of v5, /device:TPU:1, one launch (start us, length us, event | category | flops | bytes accessed | tf_op | source)
XLA Modules:
  0.0 42.6 jit_solution(12341033126416995078)
XLA Ops:
  0.0 37.1 %shard_map.46.mq_hbm = s16[2,4,4,8,16,128]{5,4,3,2,1,0:T(8,128)(2,1)} custom-call(bf16[4,2,2,1440]{3,2,1,0:T(2,128)(2,1)} %x_hbm.1), custom_call_target="tpu_custom_call" | custom-call | tf_op jit(solution)/shard_map/pallas_call | solution.py:251
  37.1 5.5 %shard_map.47 = f32[144,2,2,1152]{3,2,1,0:T(2,128)} custom-call(s32[64]{0:T(128)} %q_hbm.1, s32[64]{0:T(128)} %nu_hbm.1, s32[36,36]{1,0:T(8,128)} %kq_hbm.1, s16[2,4,4,8,16,128]{5,4,3,2,1,0:T(8,128)(2,1)} %shard_map.46.mq_hbm), custom_call_target="tpu_custom_call" | custom-call | tf_op jit(solution)/shard_map/pallas_call | solution.py:326

commit v6 on v5

--- a/solution.py
+++ b/solution.py
@@ -164,12 +164,11 @@
         left_im = jnp.where(real, pltpu.roll(left, 120, 1), pltpu.roll(left, 8, 1))
         right = jnp.concatenate([hb[v // NL, at * NL + v % NL] for v in range(NW)], axis=0)
         add(jnp.where(is_re, left_im, left_re), right, other, n == 0)
-        if n == 2:
-            for d in (2, 1, 3, 0):
-                term(4 + d, other, d, dev(x_=x_peer[d], c_=co))
         add(jnp.where(is_re, left_re, left_im), right, part, n == 0)
     for d in (2, 1, 3):
+        term(4 + d, other, d, dev(x_=x_peer[d], c_=co))
         term(d, part, d, dev(x_=x_peer[d]))
+    term(4, other, 0, sibling)
     total = part[pl.ds(x * XT, XT)]
     for n in (4, 5, 7, 1, 3, 6, 2):
         source = dev(x_=x_from[n % 4], c_=co if n >= 4 else c)

time: 42.8 us -> 42.8 us (level)
  no operation moved by 1% of the time
where the time goes in v6:
time: 42.8 us; the launch traced here: 42.7 us
  Pallas kernels  42.7 us (100%)
    pallas_call x1, Pallas kernels, correlation(): pl.pallas_call(correlate, out_shape=jax.ShapeDtypeStruct((NC, NZ, NX, HT,...  37.2 us
    pallas_call x1, Pallas kernels, shards(): pl.pallas_call(functools.partial(select, per_dev), out_shape=jax.ShapeDty...  5.5 us

profile of v6, /device:TPU:1, one launch (start us, length us, event | category | flops | bytes accessed | tf_op | source)
XLA Modules:
  0.0 42.7 jit_solution(11603719540557810694)
XLA Ops:
  0.0 37.2 %shard_map.46.mq_hbm = s16[2,4,4,8,16,128]{5,4,3,2,1,0:T(8,128)(2,1)} custom-call(bf16[4,2,2,1440]{3,2,1,0:T(2,128)(2,1)} %x_hbm.1), custom_call_target="tpu_custom_call" | custom-call | tf_op jit(solution)/shard_map/pallas_call | solution.py:250
  37.2 5.5 %shard_map.47 = f32[144,2,2,1152]{3,2,1,0:T(2,128)} custom-call(s32[64]{0:T(128)} %q_hbm.1, s32[64]{0:T(128)} %nu_hbm.1, s32[36,36]{1,0:T(8,128)} %kq_hbm.1, s16[2,4,4,8,16,128]{5,4,3,2,1,0:T(8,128)(2,1)} %shard_map.46.mq_hbm), custom_call_target="tpu_custom_call" | custom-call | tf_op jit(solution)/shard_map/pallas_call | solution.py:325
